TPU v7x, 32 devices: a whole 2x2x4 slice. The times are simulated.
32 devices in a mesh: slab: 2 (over y), row: 16 (over z, x, core).
Axes of the slice: x: 2, y: 2, z: 4, core: 2. Of those that a mesh axis runs over, the one named last changes fastest.
Arguments:
- rows_strip: bfloat16 [32, 2, 2, 3, 16, 512], P(('slab', 'row')), parts along dimension 0, may hold values from 0 to 1
- cols_strip: bfloat16 [32, 2, 2, 3, 16, 512], P(('slab', 'row')), parts along dimension 0, may hold values from 0 to 1
- offsets: int32 [32, 2, 4], P(('slab', 'row')), parts along dimension 0, may hold values from 0 to 15
- extents: int32 [32, 2, 4, 2], P(('slab', 'row')), parts along dimension 0, may hold values from 0 to 512, as said below
- prior: float32 [32, 2, 3, 4, 1024], P(('slab', 'row')), parts along dimension 0, may hold values from -3 to 3
Outputs:
- colour_maps: float32 [32, 2, 3, 4, 1024], P(('slab', 'row')), parts along dimension 0
- residual: float32 [32, 2, 3, 4, 1024], P(('slab', 'row')), parts along dimension 0
There are 2 independent parts, one for each index of `slab`. A program takes and returns all parts, laid end to end along the dimension named above; each array names one. Nothing has to cross between parts.
Inputs may be any that keep to these rules, and one draw needn't show every extreme that they name: `extents`: for each tile and direction d (0 east, 1 south, 2 south-east, 3 south-west) the first entry is at most the second; for directions 2 and 3 both are at most 16.
All inputs are finite; a program needn't handle non-finite values.
Results may differ from a plain program's by a relative error of at most 0.0003.
Values may be sent and summed in bfloat16 or wider, within the bound.
A program may use at most 64 MiB of HBM per device.

v0:
```python
import functools

import jax
import jax.numpy as jnp
from jax import lax
from jax.experimental import pallas as pl
from jax.experimental.pallas import tpu as pltpu
from jax.sharding import PartitionSpec as P

G = 32
CELL = 16
NODES = G * G
SIDE = G * CELL
LANES = 128
KINDS = 22
ROWS = KINDS * 8
META = 32

F32 = jnp.float32
BF16 = jnp.bfloat16


def iota(shape, axis):
    return lax.broadcasted_iota(jnp.int32, shape, axis)


def roll(values, shift, axis):
    return pltpu.roll(values, shift % values.shape[axis], axis)


def dot_nt(first, second):
    return lax.dot_general(first, second, (((1,), (1,)), ((), ())), preferred_element_type=F32)


def dot_nn(first, second):
    return lax.dot_general(first, second, (((1,), (0,)), ((), ())), preferred_element_type=F32)


def thirds(values):
    high = values.astype(BF16)
    rest = values - high.astype(F32)
    middle = rest.astype(BF16)
    low = (rest - middle.astype(F32)).astype(BF16)
    return jnp.concatenate([high, middle, low], axis=0)


def joined(parts):
    size = parts.shape[0] // 3
    return parts[:size] + (parts[size : 2 * size] + parts[2 * size :])


def edge_matrix():
    lane = iota((LANES, NODES), 0)
    node = iota((LANES, NODES), 1)
    spot = lane & (G - 1)
    target = jnp.where(
        lane < G,
        NODES - G + spot,
        jnp.where(lane < 2 * G, spot, jnp.where(lane < 3 * G, spot * G + G - 1, spot * G)),
    )
    return jnp.where(node == target, 1.0, 0.0).astype(BF16)


def smooth(field):
    node = iota((1, NODES), 1)
    column = node & (G - 1)
    up = jnp.where(node >= G, 1.0, 0.0)
    down = jnp.where(node < NODES - G, 1.0, 0.0)
    left = jnp.where(column > 0, 1.0, 0.0)
    right = jnp.where(column < G - 1, 1.0, 0.0)
    total = (0.5 + up + down + left + right) * field
    total = total - up * roll(field, G, 1) - down * roll(field, -G, 1)
    return total - left * roll(field, 1, 1) - right * roll(field, -1, 1)


def meta_row(buffer, tile, direction, which, width):
    spot = META + tile * 12 + direction * 3 + which
    row = buffer[spot : spot + 1, :].astype(jnp.int32)
    return jnp.concatenate([row] * (width // LANES), axis=1)


def aligned(strip, offset):
    amount = jnp.broadcast_to(offset, strip.shape)
    for bit in range(4):
        strip = jnp.where((amount & (1 << bit)) != 0, roll(strip, -(1 << bit), 1), strip)
    return strip


def flat(strip):
    return strip.astype(F32).reshape(3 * CELL, strip.shape[-1])


def put_products(lhs, tile, start, x, y):
    width = x.shape[-1]
    x = x.reshape(3, CELL, width)
    y = y.reshape(3, CELL, width)
    products = jnp.concatenate(
        [
            x[0:1] * x,
            x[1:2] * x[1:],
            x[2:3] * x[2:],
            x,
            x[0:1] * y,
            x[1:2] * y,
            x[2:3] * y,
            y,
            jnp.ones((1, CELL, width), F32),
        ],
        axis=0,
    )
    sums = (products[:, :8] + products[:, 8:]).reshape(ROWS, width)
    high = sums.astype(BF16)
    lhs[tile, :ROWS, start : start + width] = high
    lhs[tile, ROWS:, start : start + width] = (sums - high.astype(F32)).astype(BF16)


def put_weights(weights, tile, start, base, at_b, offset, low, high, exists):
    place = iota((1, SIDE), 1)
    moved = place + offset
    valid = (place >= low) & (place < high) & (moved < SIDE)
    split = (moved >> 4) - (place >> 4)
    cell = (moved >> 4) if at_b else (place >> 4)
    target = jnp.where(valid, base + cell + LANES * split, -1)
    target = jnp.where(exists > 0, target, -1)
    hit = iota((2 * LANES, SIDE), 0) == jnp.broadcast_to(target, (2 * LANES, SIDE))
    weights[tile, :, start : start + SIDE] = jnp.where(hit, 1.0 / (CELL * CELL), 0.0).astype(BF16)


def put_corner_weights(weights, tile, start, lane, offset, low, high, exists):
    place = iota((1, LANES), 1)
    valid = (place >= low) & (place < high) & (place + offset < CELL)
    target = jnp.where(valid, lane, -1)
    target = jnp.where(exists > 0, target, -1)
    hit = iota((LANES, LANES), 0) == jnp.broadcast_to(target, (LANES, LANES))
    weights[tile, :, start : start + LANES] = jnp.where(hit, 1.0 / (CELL * CELL), 0.0).astype(BF16)


def folded(parts):
    parts = (parts[:ROWS] + parts[ROWS:]).reshape(KINDS, 8, parts.shape[-1])
    return jnp.broadcast_to(jnp.sum(parts, axis=1, keepdims=True), parts.shape)


def xx_kind(p, q):
    p, q = min(p, q), max(p, q)
    if p == 3:
        return 21
    if q == 3:
        return 6 + p
    return (0, 3, 5)[p] + q - p


def xy_kind(p, q):
    if p == 3 and q == 3:
        return 21
    if q == 3:
        return 6 + p
    if p == 3:
        return 18 + q
    return 9 + 3 * p + q


def pair_terms(mats, edges, below, above):
    lane = iota((8, LANES), 1)
    row = iota((8, LANES), 0)
    at_a = (lane & G) == 0
    total = jnp.zeros((32, LANES), F32)
    for q in range(4):
        rows = slice(8 * q, 8 * q + 8)
        own = edges[rows]
        other = roll(own, 4, 0)
        near = jnp.where(
            lane < G,
            roll(below[rows], -G, 1),
            jnp.where(
                lane < 2 * G,
                roll(above[rows], G, 1),
                jnp.where(lane < 3 * G, roll(other, -G, 1), roll(other, G, 1)),
            ),
        )
        moved = jnp.where(at_a, roll(near, -1, 1), roll(near, 1, 1))
        swapped = roll(near, 4, 0)
        corner = jnp.where(row < 4, roll(swapped, G - 1, 1), roll(swapped, 1 - G, 1))
        for kind, values in enumerate((own, near, moved, corner)):
            total = total + mats[kind, q] * jnp.concatenate([values] * 4, axis=0)
    return total


def by_colour(values):
    narrow = values[:, :LANES]
    for start in range(LANES, NODES, LANES):
        narrow = narrow + values[:, start : start + LANES]
    narrow = (narrow[0:8] + narrow[8:16]) + (narrow[16:24] + narrow[24:32])
    return jnp.sum(narrow + roll(narrow, 4, 0), axis=1, keepdims=True)


def per_row(values):
    return jnp.concatenate([values] * 4, axis=0)


def kernel(
    n,
    rows_ref,
    cols_ref,
    off_ref,
    ext_ref,
    prior_ref,
    x_ref,
    res_ref,
    below_ref,
    above_ref,
    head_ref,
    below_head,
    above_head,
    edge_ref,
    below_edge,
    above_edge,
    sums_ref,
    field_ref,
    lhs,
    weights,
    corner_lhs,
    corner_weights,
    mats,
    send_sem,
    recv_sem,
    sum_send,
    sum_recv,
):
    me = lax.axis_index("row")
    barrier = pltpu.get_barrier_semaphore()

    def greet(step, carry):
        pl.semaphore_signal(barrier, inc=1, device_id={"row": lax.rem(me + step, n)})
        return carry

    lax.fori_loop(1, n, greet, 0)

    has_below = jnp.where(me < n - 1, 1, 0)
    has_above = jnp.where(me > 0, 1, 0)

    field_ref[...] = jnp.zeros_like(field_ref)
    for tile in range(2):
        for colour in range(3):
            for p in range(4):
                spot = p * 8 + tile * 4 + colour
                field_ref[spot : spot + 1, :] = prior_ref[0, tile, colour, p : p + 1, :]
    row = iota((32, NODES), 0)
    unit = jnp.where(((row & 3) == (row >> 3)) & ((row & 3) < 3), 1.0, 0.0)
    rhs = 0.5 * (unit + field_ref[...])
    select = edge_matrix()
    edges = joined(dot_nt(thirds(rhs), select))
    head_ref[:META, :] = edges
    for tile in range(2):
        for direction in range(4):
            spot = META + tile * 12 + direction * 3
            numbers = (
                off_ref[0, tile, direction],
                ext_ref[0, tile, direction, 0],
                ext_ref[0, tile, direction, 1],
            )
            for which, number in enumerate(numbers):
                head_ref[spot + which : spot + which + 1, :] = jnp.full(
                    (1, LANES), number, jnp.int32
                ).astype(F32)

    pl.semaphore_wait(barrier, n - 1)

    def up(source, target, slot):
        return pltpu.make_async_remote_copy(
            src_ref=source,
            dst_ref=target,
            send_sem=send_sem.at[slot],
            recv_sem=recv_sem.at[slot],
            device_id={"row": lax.rem(me + n - 1, n)},
        )

    def down(source, target, slot):
        return pltpu.make_async_remote_copy(
            src_ref=source,
            dst_ref=target,
            send_sem=send_sem.at[slot],
            recv_sem=recv_sem.at[slot],
            device_id={"row": lax.rem(me + 1, n)},
        )

    def exchange(ups, downs, zeros_below, zeros_above):
        @pl.when(me > 0)
        def _():
            for copy in ups:
                copy.start()

        @pl.when(me < n - 1)
        def _():
            for copy in downs:
                copy.start()

        @pl.when(me == n - 1)
        def _():
            for ref in zeros_below:
                ref[...] = jnp.zeros_like(ref)

        @pl.when(me == 0)
        def _():
            for ref in zeros_above:
                ref[...] = jnp.zeros_like(ref)

    def arrive(ups, downs):
        @pl.when(me < n - 1)
        def _():
            for copy in ups:
                copy.wait_recv()

        @pl.when(me > 0)
        def _():
            for copy in downs:
                copy.wait_recv()

    def leave(ups, downs):
        @pl.when(me > 0)
        def _():
            for copy in ups:
                copy.wait_send()

        @pl.when(me < n - 1)
        def _():
            for copy in downs:
                copy.wait_send()

    ups = (up(rows_ref.at[0, :, 0], below_ref, 0), up(head_ref, below_head, 1))
    downs = (down(rows_ref.at[0, :, 1], above_ref, 2), down(head_ref, above_head, 3))
    exchange(ups, downs, (below_ref, below_head), (above_ref, above_head))

    offset = meta_row(head_ref, 0, 0, 0, SIDE)
    low = meta_row(head_ref, 0, 0, 1, SIDE)
    high = meta_row(head_ref, 0, 0, 2, SIDE)
    east_a = flat(cols_ref[0, 0, 1])
    east_b = aligned(flat(cols_ref[0, 1, 0]), offset)
    put_products(lhs, 0, 0, east_a, east_b)
    put_products(lhs, 1, 0, east_b, east_a)
    put_weights(weights, 0, 0, 2 * G, False, offset, low, high, 1)
    put_weights(weights, 1, 0, 3 * G, True, offset, low, high, 1)
    for tile in range(2):
        offset = meta_row(head_ref, tile, 1, 0, SIDE)
        low = meta_row(head_ref, tile, 1, 1, SIDE)
        high = meta_row(head_ref, tile, 1, 2, SIDE)
        put_weights(weights, tile, SIDE, 0, False, offset, low, high, has_below)
    image = smooth(rhs)

    arrive(ups, downs)
    last = slice(SIDE - LANES, SIDE)
    first = slice(0, LANES)
    for tile in range(2):
        offset = meta_row(head_ref, tile, 1, 0, SIDE)
        south_a = flat(rows_ref[0, tile, 1])
        south_b = aligned(flat(below_ref[tile]), offset)
        put_products(lhs, tile, SIDE, south_a, south_b)

        offset = meta_row(above_head, tile, 1, 0, SIDE)
        low = meta_row(above_head, tile, 1, 1, SIDE)
        high = meta_row(above_head, tile, 1, 2, SIDE)
        north_a = flat(above_ref[tile])
        north_b = aligned(flat(rows_ref[0, tile, 0]), offset)
        put_products(lhs, tile, 2 * SIDE, north_b, north_a)
        put_weights(weights, tile, 2 * SIDE, G, True, offset, low, high, has_above)

        direction = 2 + tile
        offset = meta_row(head_ref, tile, direction, 0, LANES)
        low = meta_row(head_ref, tile, direction, 1, LANES)
        high = meta_row(head_ref, tile, direction, 2, LANES)
        if tile == 0:
            corner_a = roll(flat(rows_ref[0, 0, 1, :, :, last]), CELL, 1)
            corner_b = flat(below_ref[1, :, :, first])
        else:
            corner_a = flat(rows_ref[0, 1, 1, :, :, first])
            corner_b = roll(flat(below_ref[0, :, :, last]), CELL, 1)
        put_products(corner_lhs, tile, 0, corner_a, aligned(corner_b, offset))
        spot = G - 1 if tile == 0 else 0
        put_corner_weights(corner_weights, tile, 0, spot, offset, low, high, has_below)

        direction = 3 - tile
        offset = meta_row(above_head, 1 - tile, direction, 0, LANES)
        low = meta_row(above_head, 1 - tile, direction, 1, LANES)
        high = meta_row(above_head, 1 - tile, direction, 2, LANES)
        if tile == 0:
            corner_a = flat(above_ref[1, :, :, first])
            corner_b = roll(flat(rows_ref[0, 0, 0, :, :, last]), CELL, 1)
        else:
            corner_a = roll(flat(above_ref[0, :, :, last]), CELL, 1)
            corner_b = flat(rows_ref[0, 1, 0, :, :, first])
        put_products(corner_lhs, tile, LANES, aligned(corner_b, offset), corner_a)
        spot = 2 * G - 1 if tile == 0 else G
        put_corner_weights(corner_weights, tile, LANES, spot, offset, low, high, has_above)

    plain = [folded(dot_nt(lhs[tile], weights[tile])) for tile in range(2)]
    extra = [folded(dot_nt(corner_lhs[tile], corner_weights[tile])) for tile in range(2)]
    top = iota((KINDS, 8, LANES), 1) < 4
    none = jnp.where(top, plain[0][..., :LANES], plain[1][..., :LANES])
    one = jnp.where(top, plain[0][..., LANES:], plain[1][..., LANES:])
    corner = jnp.where(top, extra[0], extra[1])
    whole = none + one + corner
    for q in range(4):
        for kind, values, index in (
            (0, whole, xx_kind),
            (1, -none, xy_kind),
            (2, -one, xy_kind),
            (3, -corner, xy_kind),
        ):
            mats[kind, q] = jnp.concatenate([values[index(p, q)] for p in range(4)], axis=0)

    terms = pair_terms(mats, edges, below_head[:META, :], above_head[:META, :])
    image = image + joined(dot_nn(thirds(terms), select))
    edges = joined(dot_nt(thirds(image), select))
    edge_ref[...] = edges
    ups_edge = (up(edge_ref, below_edge, 4),)
    downs_edge = (down(edge_ref, above_edge, 5),)
    exchange(ups_edge, downs_edge, (below_edge,), (above_edge,))

    lane8 = iota((8, LANES), 1)

    def packed(values):
        total = jnp.zeros((8, LANES), F32)
        for spot, value in enumerate(values):
            total = jnp.where(lane8 == spot, value, total)
        return total

    def sum_copy(phase, step, owner):
        return pltpu.make_async_remote_copy(
            src_ref=sums_ref.at[phase, me],
            dst_ref=sums_ref.at[phase, owner],
            send_sem=sum_send.at[phase, step],
            recv_sem=sum_recv.at[phase, step],
            device_id={"row": lax.rem(me + step, n)},
        )

    def sums_start(phase, values):
        sums_ref[phase, me] = values

        def send(step, carry):
            sum_copy(phase, step, me).start()
            return carry

        lax.fori_loop(1, n, send, 0)

    def sums_end(phase):
        def receive(step, carry):
            sum_copy(phase, step, lax.rem(me + n - step, n)).wait_recv()
            return carry

        lax.fori_loop(1, n, receive, 0)
        return jnp.sum(sums_ref[phase], axis=0)

    sums_start(0, packed((by_colour(rhs * rhs), by_colour(rhs * image))))

    second = smooth(image)
    arrive(ups_edge, downs_edge)
    terms = pair_terms(mats, edges, below_edge[...], above_edge[...])
    second = second + joined(dot_nn(thirds(terms), select))

    real = (iota((8, 1), 0) & 3) < 3
    sums = sums_end(0)
    norm = jnp.where(real, sums[:, 0:1], 1.0)
    curvature = jnp.where(real, sums[:, 1:2], 1.0)
    alpha = norm / curvature
    step = per_row(alpha)
    residual = rhs - step * image
    lifted = image - step * second
    sums_start(
        1,
        packed(
            (
                by_colour(residual * residual),
                by_colour(residual * lifted),
                by_colour(residual * image),
            )
        ),
    )
    sums = sums_end(1)
    norm_next = jnp.where(real, sums[:, 0:1], 1.0)
    beta = norm_next / norm
    bend = sums[:, 1:2] + 2.0 * beta * sums[:, 2:3] + beta * beta * curvature
    alpha_next = norm_next / jnp.where(real, bend, 1.0)
    turn = per_row(beta)
    step_next = per_row(alpha_next)
    answer = step * rhs + step_next * (residual + turn * rhs)
    left = residual - step_next * (lifted + turn * image)
    for tile in range(2):
        for colour in range(3):
            for p in range(4):
                spot = p * 8 + tile * 4 + colour
                x_ref[0, tile, colour, p : p + 1, :] = answer[spot : spot + 1]
                res_ref[0, tile, colour, p : p + 1, :] = left[spot : spot + 1]

    leave(ups, downs)
    leave(ups_edge, downs_edge)

    def sent(step, carry):
        sum_copy(0, step, me).wait_send()
        sum_copy(1, step, me).wait_send()
        return carry

    lax.fori_loop(1, n, sent, 0)


def on_device(n, rows_strip, cols_strip, offsets, extents, prior):
    vmem = pl.BlockSpec(memory_space=pltpu.VMEM)
    smem = pl.BlockSpec(memory_space=pltpu.SMEM)
    shape = jax.ShapeDtypeStruct(prior.shape, F32)
    margins = rows_strip.shape[1:2] + rows_strip.shape[3:]
    return pl.pallas_call(
        functools.partial(kernel, n),
        out_shape=(shape, shape),
        in_specs=[vmem, vmem, smem, smem, vmem],
        out_specs=(vmem, vmem),
        scratch_shapes=[
            pltpu.VMEM(margins, BF16),
            pltpu.VMEM(margins, BF16),
            pltpu.VMEM((META + 24, LANES), F32),
            pltpu.VMEM((META + 24, LANES), F32),
            pltpu.VMEM((META + 24, LANES), F32),
            pltpu.VMEM((META, LANES), F32),
            pltpu.VMEM((META, LANES), F32),
            pltpu.VMEM((META, LANES), F32),
            pltpu.VMEM((2, n, 8, LANES), F32),
            pltpu.VMEM((32, NODES), F32),
            pltpu.VMEM((2, 2 * ROWS, 3 * SIDE), BF16),
            pltpu.VMEM((2, 2 * LANES, 3 * SIDE), BF16),
            pltpu.VMEM((2, 2 * ROWS, 2 * LANES), BF16),
            pltpu.VMEM((2, LANES, 2 * LANES), BF16),
            pltpu.VMEM((4, 4, 32, LANES), F32),
            pltpu.SemaphoreType.DMA((6,)),
            pltpu.SemaphoreType.DMA((6,)),
            pltpu.SemaphoreType.DMA((2, n)),
            pltpu.SemaphoreType.DMA((2, n)),
        ],
        compiler_params=pltpu.CompilerParams(
            collective_id=0, has_side_effects=True, vmem_limit_bytes=48 * 1024 * 1024
        ),
    )(rows_strip, cols_strip, offsets, extents, prior)


def solution(mesh):
    return jax.shard_map(
        functools.partial(on_device, mesh.shape["row"]),
        mesh=mesh,
        in_specs=(
            P(("slab", "row"), None, None, None, None, None),
            P(("slab", "row"), None, None, None, None, None),
            P(("slab", "row"), None, None),
            P(("slab", "row"), None, None, None),
            P(("slab", "row"), None, None, None, None),
        ),
        out_specs=(
            P(("slab", "row"), None, None, None, None),
            P(("slab", "row"), None, None, None, None),
        ),
        check_vma=False,
    )
```

profile of v0, /device:TPU:0, one launch (start us, length us, event | category | flops | bytes accessed | tf_op | source)
XLA Modules:
  0.0 28.2 jit_solution(12391871764150660955)
XLA Ops:
  0.6 0.0 copy-start.3
  0.6 0.8 %copy.7.ext_ref = s32[1,2,4,2]{3,2,1,0:T(4,128)S(1)} copy(s32[1,2,4,2]{2,3,1,0:T(2,128)} %param.8) | data formatting | bytes 128 | tf_op args[3]
  1.4 0.0 copy-done.3
  1.4 0.0 copy-start
  1.4 0.9 %copy-done = bf16[1,2,2,3,16,512]{5,4,3,2,1,0:T(8,128)(2,1)S(1)} copy-done((bf16[1,2,2,3,16,512]{5,4,3,2,1,0:T(8,128)(2,1)S(1)}, bf16[1,2,2,3,16,512]{5,4,3,2,1,0:T(8,128)(2,1)}, u32[]{:S(2)}) %copy-start) | copy-done | bytes 196632
  2.4 0.0 copy-start.1
  2.4 0.9 %copy-done.1 = bf16[1,2,2,3,16,512]{5,4,3,2,1,0:T(8,128)(2,1)S(1)} copy-done((bf16[1,2,2,3,16,512]{5,4,3,2,1,0:T(8,128)(2,1)S(1)}, bf16[1,2,2,3,16,512]{5,4,3,2,1,0:T(8,128)(2,1)}, u32[]{:S(2)}) %copy-start.1) | copy-done | bytes 196632
  3.3 0.0 copy-start.2
  3.3 0.9 %copy-done.2 = f32[1,2,3,4,1024]{4,3,2,1,0:T(4,128)S(1)} copy-done((f32[1,2,3,4,1024]{4,3,2,1,0:T(4,128)S(1)}, f32[1,2,3,4,1024]{4,3,2,1,0:T(4,128)}, u32[]{:S(2)}) %copy-start.2) | copy-done | bytes 98328
  4.2 22.8 %shard_map.68 = (f32[1,2,3,4,1024]{4,3,2,1,0:T(4,128)S(1)}, f32[1,2,3,4,1024]{4,3,2,1,0:T(4,128)S(1)}) custom-call(bf16[1,2,2,3,16,512]{5,4,3,2,1,0:T(8,128)(2,1)S(1)} %copy-done, bf16[1,2,2,3,16,512]{5,4,3,2,1,0:T(8,128)(2,1)S(1)} %copy-done.1, s32[1,2,4]{2,1,0:T(2,128)S(1)} %copy-done.3, s32[1,2,4,2]{3,2,1,0:T(4,128)S(1)} %copy.7.ext_ref, ...), custom_call_target="tpu_custom_call" | custom-call | tf_op jit(solution)/shard_map/pallas_call | solution.py:509
  27.0 0.6 %copy.10 = f32[1,2,3,4,1024]{4,3,2,1,0:T(4,128)} copy(f32[1,2,3,4,1024]{4,3,2,1,0:T(4,128)S(1)} %get-tuple-element.4) | data formatting | bytes 196608
  27.6 0.6 %copy.11 = f32[1,2,3,4,1024]{4,3,2,1,0:T(4,128)} copy(f32[1,2,3,4,1024]{4,3,2,1,0:T(4,128)S(1)} %get-tuple-element.5) | data formatting | bytes 196608
Async XLA Ops:
  0.6 0.8 %copy-start.3 = (s32[1,2,4]{2,1,0:T(2,128)S(1)}, s32[1,2,4]{2,1,0:T(2,128)}, u32[]{:S(2)}) copy-start(s32[1,2,4]{2,1,0:T(2,128)} %off_ref.1) | copy-start | bytes 100
  1.4 0.9 %copy-start = (bf16[1,2,2,3,16,512]{5,4,3,2,1,0:T(8,128)(2,1)S(1)}, bf16[1,2,2,3,16,512]{5,4,3,2,1,0:T(8,128)(2,1)}, u32[]{:S(2)}) copy-start(bf16[1,2,2,3,16,512]{5,4,3,2,1,0:T(8,128)(2,1)} %rows_ref.1) | copy-start | bytes 589828
  2.4 0.9 %copy-start.1 = (bf16[1,2,2,3,16,512]{5,4,3,2,1,0:T(8,128)(2,1)S(1)}, bf16[1,2,2,3,16,512]{5,4,3,2,1,0:T(8,128)(2,1)}, u32[]{:S(2)}) copy-start(bf16[1,2,2,3,16,512]{5,4,3,2,1,0:T(8,128)(2,1)} %cols_ref.1) | copy-start | bytes 589828
  3.3 0.9 %copy-start.2 = (f32[1,2,3,4,1024]{4,3,2,1,0:T(4,128)S(1)}, f32[1,2,3,4,1024]{4,3,2,1,0:T(4,128)}, u32[]{:S(2)}) copy-start(f32[1,2,3,4,1024]{4,3,2,1,0:T(4,128)} %prior_ref.1) | copy-start | bytes 294916
where the time goes:
time: 28.5 us; the launch traced here: 28.2 us
  Pallas kernels  22.8 us (80%)
  local copies, waits for them, and re-layouts  4.81 us (17%)
  between operations  0.65 us (2%)
    pallas_call x1, Pallas kernels, on_device(): pl.pallas_call(functools.partial(kernel, n), out_shape=(shape, shape), in...  22.8 us
    unnamed x11, local copies, waits for them, and re-layouts  4.81 us

commit v1 on v0

--- a/solution.py
+++ b/solution.py
@@ -215,6 +215,10 @@
     below_edge,
     above_edge,
     sums_ref,
+    rows_here,
+    east_near,
+    east_far,
+    prior_here,
     field_ref,
     lhs,
     weights,
@@ -225,6 +229,7 @@
     recv_sem,
     sum_send,
     sum_recv,
+    load_sem,
 ):
     me = lax.axis_index("row")
     barrier = pltpu.get_barrier_semaphore()
@@ -235,35 +240,22 @@
 
     lax.fori_loop(1, n, greet, 0)
 
+    loads = [
+        pltpu.make_async_copy(source, target, load_sem.at[slot])
+        for slot, (source, target) in enumerate(
+            (
+                (prior_ref.at[0], prior_here),
+                (cols_ref.at[0, 0, 1], east_near),
+                (cols_ref.at[0, 1, 0], east_far),
+                (rows_ref.at[0], rows_here),
+            )
+        )
+    ]
+    for load in loads:
+        load.start()
+
     has_below = jnp.where(me < n - 1, 1, 0)
     has_above = jnp.where(me > 0, 1, 0)
-
-    field_ref[...] = jnp.zeros_like(field_ref)
-    for tile in range(2):
-        for colour in range(3):
-            for p in range(4):
-                spot = p * 8 + tile * 4 + colour
-                field_ref[spot : spot + 1, :] = prior_ref[0, tile, colour, p : p + 1, :]
-    row = iota((32, NODES), 0)
-    unit = jnp.where(((row & 3) == (row >> 3)) & ((row & 3) < 3), 1.0, 0.0)
-    rhs = 0.5 * (unit + field_ref[...])
-    select = edge_matrix()
-    edges = joined(dot_nt(thirds(rhs), select))
-    head_ref[:META, :] = edges
-    for tile in range(2):
-        for direction in range(4):
-            spot = META + tile * 12 + direction * 3
-            numbers = (
-                off_ref[0, tile, direction],
-                ext_ref[0, tile, direction, 0],
-                ext_ref[0, tile, direction, 1],
-            )
-            for which, number in enumerate(numbers):
-                head_ref[spot + which : spot + which + 1, :] = jnp.full(
-                    (1, LANES), number, jnp.int32
-                ).astype(F32)
-
-    pl.semaphore_wait(barrier, n - 1)
 
     def up(source, target, slot):
         return pltpu.make_async_remote_copy(
@@ -326,15 +318,50 @@
             for copy in downs:
                 copy.wait_send()
 
-    ups = (up(rows_ref.at[0, :, 0], below_ref, 0), up(head_ref, below_head, 1))
-    downs = (down(rows_ref.at[0, :, 1], above_ref, 2), down(head_ref, above_head, 3))
-    exchange(ups, downs, (below_ref, below_head), (above_ref, above_head))
+    select = edge_matrix()
+    field_ref[...] = jnp.zeros_like(field_ref)
+    pl.semaphore_wait(barrier, n - 1)
+    ups_wide = (up(rows_ref.at[0, :, 0], below_ref, 0),)
+    downs_wide = (down(rows_ref.at[0, :, 1], above_ref, 2),)
+    exchange(ups_wide, downs_wide, (below_ref,), (above_ref,))
+
+    loads[0].wait()
+    for tile in range(2):
+        for colour in range(3):
+            for p in range(4):
+                spot = p * 8 + tile * 4 + colour
+                field_ref[spot : spot + 1, :] = prior_here[tile, colour, p : p + 1, :]
+    row = iota((32, NODES), 0)
+    unit = jnp.where(((row & 3) == (row >> 3)) & ((row & 3) < 3), 1.0, 0.0)
+    rhs = 0.5 * (unit + field_ref[...])
+    edges = joined(dot_nt(thirds(rhs), select))
+    head_ref[:META, :] = edges
+    for tile in range(2):
+        for direction in range(4):
+            spot = META + tile * 12 + direction * 3
+            numbers = (
+                off_ref[0, tile, direction],
+                ext_ref[0, tile, 0, direction],
+                ext_ref[0, tile, 1, direction],
+            )
+            for which, number in enumerate(numbers):
+                head_ref[spot + which : spot + which + 1, :] = jnp.full(
+                    (1, LANES), number, jnp.int32
+                ).astype(F32)
+
+    ups = (up(head_ref, below_head, 1),)
+    downs = (down(head_ref, above_head, 3),)
+    exchange(ups, downs, (below_head,), (above_head,))
+    ups = ups + ups_wide
+    downs = downs + downs_wide
 
     offset = meta_row(head_ref, 0, 0, 0, SIDE)
     low = meta_row(head_ref, 0, 0, 1, SIDE)
     high = meta_row(head_ref, 0, 0, 2, SIDE)
-    east_a = flat(cols_ref[0, 0, 1])
-    east_b = aligned(flat(cols_ref[0, 1, 0]), offset)
+    loads[1].wait()
+    loads[2].wait()
+    east_a = flat(east_near[...])
+    east_b = aligned(flat(east_far[...]), offset)
     put_products(lhs, 0, 0, east_a, east_b)
     put_products(lhs, 1, 0, east_b, east_a)
     put_weights(weights, 0, 0, 2 * G, False, offset, low, high, 1)
@@ -346,12 +373,13 @@
         put_weights(weights, tile, SIDE, 0, False, offset, low, high, has_below)
     image = smooth(rhs)
 
+    loads[3].wait()
     arrive(ups, downs)
     last = slice(SIDE - LANES, SIDE)
     first = slice(0, LANES)
     for tile in range(2):
         offset = meta_row(head_ref, tile, 1, 0, SIDE)
-        south_a = flat(rows_ref[0, tile, 1])
+        south_a = flat(rows_here[tile, 1])
         south_b = aligned(flat(below_ref[tile]), offset)
         put_products(lhs, tile, SIDE, south_a, south_b)
 
@@ -359,7 +387,7 @@
         low = meta_row(above_head, tile, 1, 1, SIDE)
         high = meta_row(above_head, tile, 1, 2, SIDE)
         north_a = flat(above_ref[tile])
-        north_b = aligned(flat(rows_ref[0, tile, 0]), offset)
+        north_b = aligned(flat(rows_here[tile, 0]), offset)
         put_products(lhs, tile, 2 * SIDE, north_b, north_a)
         put_weights(weights, tile, 2 * SIDE, G, True, offset, low, high, has_above)
 
@@ -368,10 +396,10 @@
         low = meta_row(head_ref, tile, direction, 1, LANES)
         high = meta_row(head_ref, tile, direction, 2, LANES)
         if tile == 0:
-            corner_a = roll(flat(rows_ref[0, 0, 1, :, :, last]), CELL, 1)
+            corner_a = roll(flat(rows_here[0, 1, :, :, last]), CELL, 1)
             corner_b = flat(below_ref[1, :, :, first])
         else:
-            corner_a = flat(rows_ref[0, 1, 1, :, :, first])
+            corner_a = flat(rows_here[1, 1, :, :, first])
             corner_b = roll(flat(below_ref[0, :, :, last]), CELL, 1)
         put_products(corner_lhs, tile, 0, corner_a, aligned(corner_b, offset))
         spot = G - 1 if tile == 0 else 0
@@ -383,10 +411,10 @@
         high = meta_row(above_head, 1 - tile, direction, 2, LANES)
         if tile == 0:
             corner_a = flat(above_ref[1, :, :, first])
-            corner_b = roll(flat(rows_ref[0, 0, 0, :, :, last]), CELL, 1)
+            corner_b = roll(flat(rows_here[0, 0, :, :, last]), CELL, 1)
         else:
             corner_a = roll(flat(above_ref[0, :, :, last]), CELL, 1)
-            corner_b = flat(rows_ref[0, 1, 0, :, :, first])
+            corner_b = flat(rows_here[1, 0, :, :, first])
         put_products(corner_lhs, tile, LANES, aligned(corner_b, offset), corner_a)
         spot = 2 * G - 1 if tile == 0 else G
         put_corner_weights(corner_weights, tile, LANES, spot, offset, low, high, has_above)
@@ -415,72 +443,76 @@
     downs_edge = (down(edge_ref, above_edge, 5),)
     exchange(ups_edge, downs_edge, (below_edge,), (above_edge,))
 
-    lane8 = iota((8, LANES), 1)
-
-    def packed(values):
-        total = jnp.zeros((8, LANES), F32)
-        for spot, value in enumerate(values):
-            total = jnp.where(lane8 == spot, value, total)
-        return total
-
-    def sum_copy(phase, step, owner):
-        return pltpu.make_async_remote_copy(
-            src_ref=sums_ref.at[phase, me],
-            dst_ref=sums_ref.at[phase, owner],
-            send_sem=sum_send.at[phase, step],
-            recv_sem=sum_recv.at[phase, step],
-            device_id={"row": lax.rem(me + step, n)},
-        )
-
-    def sums_start(phase, values):
-        sums_ref[phase, me] = values
-
-        def send(step, carry):
-            sum_copy(phase, step, me).start()
-            return carry
-
-        lax.fori_loop(1, n, send, 0)
-
-    def sums_end(phase):
-        def receive(step, carry):
-            sum_copy(phase, step, lax.rem(me + n - step, n)).wait_recv()
-            return carry
-
-        lax.fori_loop(1, n, receive, 0)
-        return jnp.sum(sums_ref[phase], axis=0)
-
-    sums_start(0, packed((by_colour(rhs * rhs), by_colour(rhs * image))))
+    lane = iota((8, LANES), 1)
+    row = iota((8, LANES), 0)
+    spread = (lane == (row & 3)) & (lane < 3)
+
+    def as_row(column):
+        return jnp.sum(jnp.where(spread & (row < 4), column, 0.0), axis=0, keepdims=True)
+
+    def as_column(values):
+        column = jnp.sum(jnp.where(spread, values, 0.0), axis=1, keepdims=True)
+        return jnp.concatenate([column] * 4, axis=0)
+
+    rr = by_colour(rhs * rhs)
+    rq = by_colour(rhs * image)
+    theta = jnp.clip(jnp.where(rr > 0.0, rq / jnp.where(rr > 0.0, rr, 1.0), 0.0), 0.0, 20.0)
+    tilt = per_row(theta)
+    bent = image - tilt * rhs
+    ru = by_colour(rhs * bent)
+    uu = by_colour(bent * bent)
 
     second = smooth(image)
     arrive(ups_edge, downs_edge)
     terms = pair_terms(mats, edges, below_edge[...], above_edge[...])
     second = second + joined(dot_nn(thirds(terms), select))
-
-    real = (iota((8, 1), 0) & 3) < 3
-    sums = sums_end(0)
-    norm = jnp.where(real, sums[:, 0:1], 1.0)
-    curvature = jnp.where(real, sums[:, 1:2], 1.0)
+    twice = second - tilt * image
+    rv = by_colour(rhs * twice)
+    uv = by_colour(bent * twice)
+    parts = [as_row(value) for value in (rr, rq, ru, uu, rv, uv, theta)]
+    sums_ref[me] = jnp.concatenate(parts + [jnp.zeros((1, LANES), F32)], axis=0)
+
+    def sum_copy(step, owner):
+        return pltpu.make_async_remote_copy(
+            src_ref=sums_ref.at[me],
+            dst_ref=sums_ref.at[owner],
+            send_sem=sum_send.at[step],
+            recv_sem=sum_recv.at[step],
+            device_id={"row": lax.rem(me + step, n)},
+        )
+
+    def send(step, carry):
+        sum_copy(step, me).start()
+        return carry
+
+    def receive(step, carry):
+        sum_copy(step, lax.rem(me + n - step, n)).wait_recv()
+        return carry
+
+    lax.fori_loop(1, n, send, 0)
+    lax.fori_loop(1, n, receive, 0)
+    rr, rq, ru, uu, rv, uv, theta = [sums_ref[:, spot, :] for spot in range(7)]
+
+    def total(values):
+        return jnp.sum(values, axis=0, keepdims=True)
+
+    real = iota((1, LANES), 1) < 3
+    norm = jnp.where(real, total(rr), 1.0)
+    curvature = jnp.where(real, total(rq), 1.0)
     alpha = norm / curvature
-    step = per_row(alpha)
+    keep = 1.0 - alpha * theta
+    uq = uu + theta * ru
+    norm_next = total(keep * keep * rr - 2.0 * alpha * keep * ru + alpha * alpha * uu)
+    with_image = total(keep * rq - alpha * uq)
+    with_lifted = total(keep * keep * rq - alpha * keep * (rv + uq) + alpha * alpha * uv)
+    beta = norm_next / norm
+    bend = with_lifted + 2.0 * beta * with_image + beta * beta * curvature
+    alpha_next = norm_next / jnp.where(real, bend, 1.0)
+    step = as_column(alpha)
+    step_next = as_column(alpha_next)
+    turn = as_column(beta)
     residual = rhs - step * image
     lifted = image - step * second
-    sums_start(
-        1,
-        packed(
-            (
-                by_colour(residual * residual),
-                by_colour(residual * lifted),
-                by_colour(residual * image),
-            )
-        ),
-    )
-    sums = sums_end(1)
-    norm_next = jnp.where(real, sums[:, 0:1], 1.0)
-    beta = norm_next / norm
-    bend = sums[:, 1:2] + 2.0 * beta * sums[:, 2:3] + beta * beta * curvature
-    alpha_next = norm_next / jnp.where(real, bend, 1.0)
-    turn = per_row(beta)
-    step_next = per_row(alpha_next)
     answer = step * rhs + step_next * (residual + turn * rhs)
     left = residual - step_next * (lifted + turn * image)
     for tile in range(2):
@@ -494,8 +526,7 @@
     leave(ups_edge, downs_edge)
 
     def sent(step, carry):
-        sum_copy(0, step, me).wait_send()
-        sum_copy(1, step, me).wait_send()
+        sum_copy(step, me).wait_send()
         return carry
 
     lax.fori_loop(1, n, sent, 0)
@@ -503,13 +534,14 @@
 
 def on_device(n, rows_strip, cols_strip, offsets, extents, prior):
     vmem = pl.BlockSpec(memory_space=pltpu.VMEM)
+    hbm = pl.BlockSpec(memory_space=pltpu.HBM)
     smem = pl.BlockSpec(memory_space=pltpu.SMEM)
     shape = jax.ShapeDtypeStruct(prior.shape, F32)
     margins = rows_strip.shape[1:2] + rows_strip.shape[3:]
     return pl.pallas_call(
         functools.partial(kernel, n),
         out_shape=(shape, shape),
-        in_specs=[vmem, vmem, smem, smem, vmem],
+        in_specs=[hbm, hbm, smem, smem, hbm],
         out_specs=(vmem, vmem),
         scratch_shapes=[
             pltpu.VMEM(margins, BF16),
@@ -520,7 +552,11 @@
             pltpu.VMEM((META, LANES), F32),
             pltpu.VMEM((META, LANES), F32),
             pltpu.VMEM((META, LANES), F32),
-            pltpu.VMEM((2, n, 8, LANES), F32),
+            pltpu.VMEM((n, 8, LANES), F32),
+            pltpu.VMEM(rows_strip.shape[1:], BF16),
+            pltpu.VMEM(cols_strip.shape[3:], BF16),
+            pltpu.VMEM(cols_strip.shape[3:], BF16),
+            pltpu.VMEM(prior.shape[1:], F32),
             pltpu.VMEM((32, NODES), F32),
             pltpu.VMEM((2, 2 * ROWS, 3 * SIDE), BF16),
             pltpu.VMEM((2, 2 * LANES, 3 * SIDE), BF16),
@@ -529,13 +565,14 @@
             pltpu.VMEM((4, 4, 32, LANES), F32),
             pltpu.SemaphoreType.DMA((6,)),
             pltpu.SemaphoreType.DMA((6,)),
-            pltpu.SemaphoreType.DMA((2, n)),
-            pltpu.SemaphoreType.DMA((2, n)),
+            pltpu.SemaphoreType.DMA((n,)),
+            pltpu.SemaphoreType.DMA((n,)),
+            pltpu.SemaphoreType.DMA((4,)),
         ],
         compiler_params=pltpu.CompilerParams(
             collective_id=0, has_side_effects=True, vmem_limit_bytes=48 * 1024 * 1024
         ),
-    )(rows_strip, cols_strip, offsets, extents, prior)
+    )(rows_strip, cols_strip, offsets, extents.swapaxes(2, 3), prior)
 
 
 def solution(mesh):

time: 28.5 us -> 26 us (0.912)
  Pallas kernels: 22.8 us -> 19.7 us
  local copies, waits for them, and re-layouts: 4.81 us -> 5.38 us
    pallas_call x1, Pallas kernels: 22.8 us -> 19.7 us  [on_device(): pl.pallas_call(functools.partial(kernel, n), out_shape=(shape, shape), in...]
    unnamed x11 -> x12, local copies, waits for them, and re-layouts: 4.81 us -> 5.38 us
where the time goes in v1:
time: 26 us; the launch traced here: 25.8 us
  Pallas kernels  19.7 us (76%)
  local copies, waits for them, and re-layouts  5.38 us (21%)
  between operations  0.65 us (2%)
    pallas_call x1, Pallas kernels, on_device(): pl.pallas_call(functools.partial(kernel, n), out_shape=(shape, shape), in...  19.7 us
    unnamed x12, local copies, waits for them, and re-layouts  5.38 us

profile of v1, /device:TPU:0, one launch (start us, length us, event | category | flops | bytes accessed | tf_op | source)
XLA Modules:
  0.0 25.8 jit_solution(4781644653513566242)
XLA Ops:
  0.6 0.0 copy-start.4
  0.6 0.7 %copy-done.4 = s32[1,2,4]{2,1,0:T(2,128)S(1)} copy-done((s32[1,2,4]{2,1,0:T(2,128)S(1)}, s32[1,2,4]{2,1,0:T(2,128)}, u32[]{:S(2)}) %copy-start.4) | copy-done | bytes 56
  1.3 0.0 copy-start
  1.3 0.9 %copy-done = bf16[1,2,2,3,16,512]{5,4,3,2,1,0:T(8,128)(2,1)S(1)} copy-done((bf16[1,2,2,3,16,512]{5,4,3,2,1,0:T(8,128)(2,1)S(1)}, bf16[1,2,2,3,16,512]{5,4,3,2,1,0:T(8,128)(2,1)}, u32[]{:S(2)}) %copy-start) | copy-done | bytes 196632
  2.2 0.0 copy-start.1
  2.2 0.9 %copy-done.1 = bf16[1,2,2,3,16,512]{5,4,3,2,1,0:T(8,128)(2,1)S(1)} copy-done((bf16[1,2,2,3,16,512]{5,4,3,2,1,0:T(8,128)(2,1)S(1)}, bf16[1,2,2,3,16,512]{5,4,3,2,1,0:T(8,128)(2,1)}, u32[]{:S(2)}) %copy-start.1) | copy-done | bytes 196632
  3.2 0.0 copy-start.2
  3.2 0.9 %copy-done.2 = f32[1,2,3,4,1024]{4,3,2,1,0:T(4,128)S(1)} copy-done((f32[1,2,3,4,1024]{4,3,2,1,0:T(4,128)S(1)}, f32[1,2,3,4,1024]{4,3,2,1,0:T(4,128)}, u32[]{:S(2)}) %copy-start.2) | copy-done | bytes 98328
  4.1 0.0 copy-start.3
  4.1 0.7 %copy-done.3 = s32[1,2,4,2]{2,3,1,0:T(2,128)S(1)} copy-done((s32[1,2,4,2]{2,3,1,0:T(2,128)S(1)}, s32[1,2,4,2]{2,3,1,0:T(2,128)}, u32[]{:S(2)}) %copy-start.3) | copy-done | bytes 88
  4.7 19.7 %shard_map.68 = (f32[1,2,3,4,1024]{4,3,2,1,0:T(4,128)S(1)}, f32[1,2,3,4,1024]{4,3,2,1,0:T(4,128)S(1)}) custom-call(bf16[1,2,2,3,16,512]{5,4,3,2,1,0:T(8,128)(2,1)S(1)} %copy-done, bf16[1,2,2,3,16,512]{5,4,3,2,1,0:T(8,128)(2,1)S(1)} %copy-done.1, s32[1,2,4]{2,1,0:T(2,128)S(1)} %copy-done.4, s32[1,2,2,4]{3,2,1,0:T(2,128)S(1)} %bitcast.1, ...), custom_call_target="tpu_custom_call" | custom-call | tf_op jit(solution)/shard_map/pallas_call | solution.py:541
  24.5 0.6 %copy.9 = f32[1,2,3,4,1024]{4,3,2,1,0:T(4,128)} copy(f32[1,2,3,4,1024]{4,3,2,1,0:T(4,128)S(1)} %get-tuple-element.4) | data formatting | bytes 196608
  25.1 0.6 %copy.10 = f32[1,2,3,4,1024]{4,3,2,1,0:T(4,128)} copy(f32[1,2,3,4,1024]{4,3,2,1,0:T(4,128)S(1)} %get-tuple-element.5) | data formatting | bytes 196608
Async XLA Ops:
  0.6 0.7 %copy-start.4 = (s32[1,2,4]{2,1,0:T(2,128)S(1)}, s32[1,2,4]{2,1,0:T(2,128)}, u32[]{:S(2)}) copy-start(s32[1,2,4]{2,1,0:T(2,128)} %off_ref.1) | copy-start | bytes 100
  1.3 0.9 %copy-start = (bf16[1,2,2,3,16,512]{5,4,3,2,1,0:T(8,128)(2,1)S(1)}, bf16[1,2,2,3,16,512]{5,4,3,2,1,0:T(8,128)(2,1)}, u32[]{:S(2)}) copy-start(bf16[1,2,2,3,16,512]{5,4,3,2,1,0:T(8,128)(2,1)} %rows_ref.1) | copy-start | bytes 589828
  2.2 0.9 %copy-start.1 = (bf16[1,2,2,3,16,512]{5,4,3,2,1,0:T(8,128)(2,1)S(1)}, bf16[1,2,2,3,16,512]{5,4,3,2,1,0:T(8,128)(2,1)}, u32[]{:S(2)}) copy-start(bf16[1,2,2,3,16,512]{5,4,3,2,1,0:T(8,128)(2,1)} %cols_ref.1) | copy-start | bytes 589828
  3.2 0.9 %copy-start.2 = (f32[1,2,3,4,1024]{4,3,2,1,0:T(4,128)S(1)}, f32[1,2,3,4,1024]{4,3,2,1,0:T(4,128)}, u32[]{:S(2)}) copy-start(f32[1,2,3,4,1024]{4,3,2,1,0:T(4,128)} %prior_ref.1) | copy-start | bytes 294916
  4.1 0.7 %copy-start.3 = (s32[1,2,4,2]{2,3,1,0:T(2,128)S(1)}, s32[1,2,4,2]{2,3,1,0:T(2,128)}, u32[]{:S(2)}) copy-start(s32[1,2,4,2]{2,3,1,0:T(2,128)} %param.8) | copy-start | bytes 196

commit v2 on v1

--- a/solution.py
+++ b/solution.py
@@ -570,7 +570,7 @@
             pltpu.SemaphoreType.DMA((4,)),
         ],
         compiler_params=pltpu.CompilerParams(
-            collective_id=0, has_side_effects=True, vmem_limit_bytes=48 * 1024 * 1024
+            collective_id=0, has_side_effects=True, vmem_limit_bytes=64 * 1024 * 1024
         ),
     )(rows_strip, cols_strip, offsets, extents.swapaxes(2, 3), prior)
 

time: 26 us -> 23.8 us (0.915)
  local copies, waits for them, and re-layouts: 5.38 us -> 2.22 us
  Pallas kernels: 19.7 us -> 20.7 us
    unnamed x12 -> x4, local copies, waits for them, and re-layouts: 5.38 us -> 2.22 us
    pallas_call x1, Pallas kernels: 19.7 us -> 20.7 us  [on_device(): pl.pallas_call(functools.partial(kernel, n), out_shape=(shape, shape), in...]
where the time goes in v2:
time: 23.8 us; the launch traced here: 23.6 us
  Pallas kernels  20.7 us (87%)
  local copies, waits for them, and re-layouts  2.22 us (9%)
  between operations  0.65 us (3%)
    pallas_call x1, Pallas kernels, on_device(): pl.pallas_call(functools.partial(kernel, n), out_shape=(shape, shape), in...  20.7 us
    unnamed x4, local copies, waits for them, and re-layouts  2.22 us

profile of v2, /device:TPU:0, one launch (start us, length us, event | category | flops | bytes accessed | tf_op | source)
XLA Modules:
  0.0 23.6 jit_solution(14575401693783600828)
XLA Ops:
  0.6 20.7 %shard_map.68 = (f32[1,2,3,4,1024]{4,3,2,1,0:T(4,128)}, f32[1,2,3,4,1024]{4,3,2,1,0:T(4,128)}) custom-call(bf16[1,2,2,3,16,512]{5,4,3,2,1,0:T(8,128)(2,1)} %rows_ref.1, bf16[1,2,2,3,16,512]{5,4,3,2,1,0:T(8,128)(2,1)} %cols_ref.1, s32[1,2,4]{2,1,0:T(2,128)} %off_ref.1, s32[1,2,2,4]{3,2,1,0:T(2,128)} %bitcast.1, f32[1,2,3,4,1024]{4,3,2,1,0:T(4,128)} %prior_ref.1), custom_call_target="tpu_custom_call" | custom-call | tf_op jit(solution)/shard_map/pallas_call | solution.py:541
  21.4 0.0 copy-start
  21.4 1.6 %copy.9 = f32[1,2,3,4,1024]{4,3,2,1,0:T(4,128)} copy(f32[1,2,3,4,1024]{4,3,2,1,0:T(4,128)} %get-tuple-element.4) | data formatting | bytes 196608
  22.9 0.0 copy-done
  22.9 0.6 %copy.10 = f32[1,2,3,4,1024]{4,3,2,1,0:T(4,128)} copy(f32[1,2,3,4,1024]{4,3,2,1,0:T(4,128)S(1)} %copy-done) | data formatting | bytes 196608
Async XLA Ops:
  21.4 1.6 %copy-start = (f32[1,2,3,4,1024]{4,3,2,1,0:T(4,128)S(1)}, f32[1,2,3,4,1024]{4,3,2,1,0:T(4,128)}, u32[]{:S(2)}) copy-start(f32[1,2,3,4,1024]{4,3,2,1,0:T(4,128)} %get-tuple-element.5) | copy-start | bytes 294916

commit v3 on v2

--- a/solution.py
+++ b/solution.py
@@ -372,6 +372,7 @@
         high = meta_row(head_ref, tile, 1, 2, SIDE)
         put_weights(weights, tile, SIDE, 0, False, offset, low, high, has_below)
     image = smooth(rhs)
+    smooth_edges = joined(dot_nt(thirds(image), select))
 
     loads[3].wait()
     arrive(ups, downs)
@@ -436,12 +437,13 @@
             mats[kind, q] = jnp.concatenate([values[index(p, q)] for p in range(4)], axis=0)
 
     terms = pair_terms(mats, edges, below_head[:META, :], above_head[:META, :])
-    image = image + joined(dot_nn(thirds(terms), select))
-    edges = joined(dot_nt(thirds(image), select))
+    shared = dot_nt(select, select).astype(BF16)
+    edges = smooth_edges + joined(dot_nn(thirds(terms), shared))
     edge_ref[...] = edges
     ups_edge = (up(edge_ref, below_edge, 4),)
     downs_edge = (down(edge_ref, above_edge, 5),)
     exchange(ups_edge, downs_edge, (below_edge,), (above_edge,))
+    image = image + joined(dot_nn(thirds(terms), select))
 
     lane = iota((8, LANES), 1)
     row = iota((8, LANES), 0)

time: 23.8 us -> 23.5 us (0.987)
  no operation moved by 1% of the time
where the time goes in v3:
time: 23.5 us; the launch traced here: 23.4 us
  Pallas kernels  20.5 us (87%)
  local copies, waits for them, and re-layouts  2.22 us (9%)
  between operations  0.65 us (3%)
    pallas_call x1, Pallas kernels, on_device(): pl.pallas_call(functools.partial(kernel, n), out_shape=(shape, shape), in...  20.5 us
    unnamed x4, local copies, waits for them, and re-layouts  2.22 us

profile of v3, /device:TPU:0, one launch (start us, length us, event | category | flops | bytes accessed | tf_op | source)
XLA Modules:
  0.0 23.4 jit_solution(14053281858312141738)
XLA Ops:
  0.6 20.5 %shard_map.68 = (f32[1,2,3,4,1024]{4,3,2,1,0:T(4,128)}, f32[1,2,3,4,1024]{4,3,2,1,0:T(4,128)}) custom-call(bf16[1,2,2,3,16,512]{5,4,3,2,1,0:T(8,128)(2,1)} %rows_ref.1, bf16[1,2,2,3,16,512]{5,4,3,2,1,0:T(8,128)(2,1)} %cols_ref.1, s32[1,2,4]{2,1,0:T(2,128)} %off_ref.1, s32[1,2,2,4]{3,2,1,0:T(2,128)} %bitcast.1, f32[1,2,3,4,1024]{4,3,2,1,0:T(4,128)} %prior_ref.1), custom_call_target="tpu_custom_call" | custom-call | tf_op jit(solution)/shard_map/pallas_call | solution.py:543
  21.1 0.0 copy-start
  21.1 1.6 %copy.9 = f32[1,2,3,4,1024]{4,3,2,1,0:T(4,128)} copy(f32[1,2,3,4,1024]{4,3,2,1,0:T(4,128)} %get-tuple-element.4) | data formatting | bytes 196608
  22.7 0.0 copy-done
  22.7 0.6 %copy.10 = f32[1,2,3,4,1024]{4,3,2,1,0:T(4,128)} copy(f32[1,2,3,4,1024]{4,3,2,1,0:T(4,128)S(1)} %copy-done) | data formatting | bytes 196608
Async XLA Ops:
  21.1 1.6 %copy-start = (f32[1,2,3,4,1024]{4,3,2,1,0:T(4,128)S(1)}, f32[1,2,3,4,1024]{4,3,2,1,0:T(4,128)}, u32[]{:S(2)}) copy-start(f32[1,2,3,4,1024]{4,3,2,1,0:T(4,128)} %get-tuple-element.5) | copy-start | bytes 294916
